TPU v7x, 32 devices: a whole 2x2x4 slice. The times are simulated.
32 devices in a mesh: pair: 16 (over z, y, core), irrep: 2 (over x).
Axes of the slice: x: 2, y: 2, z: 4, core: 2. Of those that a mesh axis runs over, the one named last changes fastest.
Arguments:
- blocks: bfloat16 [16, 2, 1280, 1280], P(None, 'irrep', 'pair'), may hold values from -6 to 6
- coefficients: bfloat16 [1280, 2048], P(None, 'irrep'), may hold values from -0.15625 to 0.15625
- shell_batch_functions: int32 [1280], replicated, may hold values from 0 to 1279, each once
- irrep_counts: int32 [8], replicated, may hold values from 128 to 256, as said below
- pair_symmetry: int32 [16, 2], P('pair', 'irrep'), may hold values from 0 to 7
Outputs:
- orbital_pair_integrals: float32 [16, 2, 8, 256, 256], P('pair', 'irrep')
Inputs may be any that keep to these rules, and one draw needn't show every extreme that they name: `shell_batch_functions`: each AO function appears exactly once. `irrep_counts`: irrep 0 holds all 256 virtual orbitals.
All inputs are finite; a program needn't handle non-finite values.
Results may differ from a plain program's by a relative error of at most 0.0029.
Values may be sent and summed in bfloat16 or wider, within the bound.
A program may use at most 128 MiB of HBM per device.

v0:
```python
import jax
import jax.numpy as jnp
from jax import lax
from jax.sharding import PartitionSpec as P

NAO = 1280
VIR = 256
NIRR = 8


def mask_columns(whole, irrep_counts):
    width = whole.shape[1]
    col = jnp.arange(width, dtype=jnp.int32)
    owner = col // VIR
    irrep_labels = jnp.arange(irrep_counts.shape[0], dtype=jnp.int32)
    limit = jnp.sum(
        jnp.where(owner[:, None] == irrep_labels[None, :], irrep_counts[None, :], 0), axis=1
    )
    live = col % VIR < limit
    return jnp.where(live[None, :], whole, jnp.zeros_like(whole))


def finish_pairs(moved, third_row_group, symmetry):

    def one_pair(half, sym_value):
        half_three = half.reshape(half.shape[0], NIRR, VIR)
        partner_irrep = jnp.bitwise_xor(jnp.arange(NIRR, dtype=jnp.int32), sym_value)
        selected_option = jnp.take(half_three, partner_irrep, axis=1)
        return jnp.einsum(
            "ytq,ytj->tqj", third_row_group, selected_option, preferred_element_type=jnp.float32
        )

    return jax.vmap(one_pair)(moved, symmetry)


def body(blocks, coefficients, shell_batch_functions, irrep_counts, pair_symmetry):
    pairs_here = blocks.shape[0]
    batch_rows = blocks.shape[2]
    whole = lax.all_gather(coefficients, "irrep", axis=1, tiled=True)
    masked = mask_columns(whole, irrep_counts)
    third_row_group = jnp.take(masked, shell_batch_functions, axis=0).reshape(NAO, NIRR, VIR)
    gathered = lax.all_to_all(
        blocks.reshape(pairs_here, batch_rows, NAO), "pair", split_axis=0, concat_axis=1, tiled=True
    )
    local_pair_list = gathered.shape[0]
    moved = jnp.dot(
        gathered.reshape(local_pair_list * NAO, NAO), masked, preferred_element_type=jnp.float32
    ).astype(jnp.bfloat16)
    moved = moved.reshape(local_pair_list, NAO, NIRR * VIR)
    result = finish_pairs(moved, third_row_group, pair_symmetry[:, 0])
    return result[:, None]


def solution(mesh):
    in_specs = (P(None, "irrep", "pair", None), P(None, "irrep"), P(), P(), P("pair", "irrep"))
    out_specs = P("pair", "irrep", None, None, None)
    return jax.shard_map(body, mesh=mesh, in_specs=in_specs, out_specs=out_specs, check_vma=False)
```

profile of v0, /device:TPU:0, one launch (start us, length us, event | category | flops | bytes accessed | tf_op | source)
XLA Modules:
  0.0 145.2 jit_solution(13259157394186770481)
XLA Ops:
  6.5 0.0 copy-start
  6.5 0.0 copy-start.1
  6.5 0.0 all-gather.2.cloned.1.call-start
  6.5 0.7 all-gather.2.cloned.1.call-update
  7.3 7.4 %all-to-all-start = ((bf16[16,80,1280]{2,1,0:T(8,128)(2,1)}), bf16[16,80,1280]{2,1,0:T(8,128)(2,1)S(1)}, u32[]{:S(2)}, u32[]{:S(2)}) async-start(bf16[16,80,1280]{2,1,0:T(8,128)(2,1)} %bitcast.24), calls=%async_computation | async-start | bytes 6553600 | tf_op jit(solution)/shard_map/all_to_all | solution.py:42
  15.4 0.0 copy-done
  15.4 0.0 copy-done.1
  15.4 0.1 select_reduce_fusion
  15.5 64.7 %all-gather.2.cloned.1.call-done = bf16[1280,2048]{1,0:T(8,128)(2,1)} async-done(((bf16[1280,1024]{1,0:T(8,128)(2,1)}), bf16[1280,2048]{1,0:T(8,128)(2,1)}) %all-gather.2.cloned.1.call-update) | async-done | bytes 5242896 | tf_op jit(solution)/shard_map/all_gather | solution.py:39
  80.2 5.2 %broadcast_select_fusion = bf16[1280,2048]{1,0:T(8,128)(2,1)} fusion(bf16[1280,2048]{1,0:T(8,128)(2,1)} %all-gather.2.cloned.1.call-done, pred[2048]{0:T(1024)(128)(4,1)S(1)} %fusion.13), kind=kLoop, calls=%fused_computation.8 | loop fusion | flops 2621440 | bytes 10487808 | tf_op jit(solution)/shard_map/jit(_where)/select_n | solution.py:20
  85.4 14.0 %gather_fusion = bf16[1280,2048]{1,0:T(8,128)(2,1)} fusion(bf16[1280,2048]{1,0:T(8,128)(2,1)} %broadcast_select_fusion, s32[2048]{0:T(1024)S(1)} %pad_clamp_fusion), kind=kCustom, calls=%fused_computation | custom fusion | bytes 10490880 | tf_op jit(solution)/shard_map/jit(_take)/gather | solution.py:41
  99.4 7.9 %copy.11 = bf16[1280,2048]{0,1:T(8,128)(2,1)} copy(bf16[1280,2048]{1,0:T(8,128)(2,1)} %gather_fusion) | data formatting | bytes 10485760 | tf_op jit(solution)/shard_map/jit(_take)/gather | solution.py:41
  107.2 0.0 all-to-all-done
  107.2 10.5 %convolution_convert_fusion = bf16[2048,1280]{1,0:T(8,128)(2,1)} fusion(bf16[1280,2048]{1,0:T(8,128)(2,1)} %broadcast_select_fusion, bf16[1280,1280]{1,0:T(8,128)(2,1)S(1)} %bitcast.25), kind=kOutput, calls=%fused_computation.2 | convolution fusion | flops 6713507840 | bytes 13762560 | tf_op jit(solution)/shard_map/dot_general | solution.py:46
  117.7 7.8 %copy.10 = bf16[1,1280,8,256]{3,1,2,0:T(8,128)(2,1)} copy(bf16[1,1280,8,256]{1,3,2,0:T(8,128)(2,1)} %bitcast.23) | data formatting | bytes 10485760 | tf_op jit(solution)/shard_map/vmap()/reshape;reshape | solution.py:26
  125.5 5.7 %gather_fusion.1 = bf16[8,1280,256]{2,1,0:T(8,128)(2,1)} fusion(bf16[1,1280,8,256]{3,1,2,0:T(8,128)(2,1)} %copy.10, s32[8]{0:T(128)S(1)} %or_bitcast_fusion), kind=kCustom, calls=%fused_computation.1 | custom fusion | bytes 10485824 | tf_op jit(solution)/shard_map/vmap(jit(_take))/gather | solution.py:28
  131.2 7.1 %fusion.8 = f32[1,1,8,256,256]{4,3,2,1,0:T(8,128)} fusion(bf16[8,1280,256]{2,1,0:T(8,128)(2,1)} %gather_fusion.1, pred[8]{0:T(512)(128)(4,1)S(1)} %compare_and_fusion.1, bf16[1280,8,256]{0,2,1:T(8,128)(2,1)} %bitcast.22, pred[1280]{0:T(1024)(128)(4,1)S(1)} %compare_and_fusion), kind=kOutput, calls=%fused_computation.12 | convolution fusion | flops 1347420160 | bytes 12584200 | tf_op jit(solution)/shard_map/vmap(ytq,ytj->tqj)/dot_general | solution.py:29
  (9 shorter events, 0.1 us)
Async XLA Ops:
  6.5 8.8 %copy-start = (s32[1280]{0:T(1024)S(1)}, s32[1280]{0:T(1024)}, u32[]{:S(2)}) copy-start(s32[1280]{0:T(1024)} %param.7) | copy-start | bytes 15364
  6.5 8.9 %copy-start.1 = (s32[8]{0:T(128)S(1)}, s32[8]{0:T(128)}, u32[]{:S(2)}) copy-start(s32[8]{0:T(128)} %param.8) | copy-start | bytes 100
  6.5 73.7 %all-gather.2.cloned.1.call-start = ((), (), s32[]{:S(2)}) async-start(), calls=%async_computation.1 | async-start | bytes 7864320 | tf_op jit(solution)/shard_map/all_gather | solution.py:39
  7.3 100.0 %all-to-all-start = ((bf16[16,80,1280]{2,1,0:T(8,128)(2,1)}), bf16[16,80,1280]{2,1,0:T(8,128)(2,1)S(1)}, u32[]{:S(2)}, u32[]{:S(2)}) async-start(bf16[16,80,1280]{2,1,0:T(8,128)(2,1)} %bitcast.24), calls=%async_computation | async-start | bytes 6553600 | tf_op jit(solution)/shard_map/all_to_all | solution.py:42
Sparse Core Ops, SparseCore 0:
  8.9 71.2 all-gather.1
where the time goes:
time: 146 us; the launch traced here: 145 us
  waiting for transfers between devices  65.4 us (45%)
  local copies, waits for them, and re-layouts  35.4 us (24%)
  matrix products  17.5 us (12%)
  between operations  14.1 us (10%)
  starting transfers between devices  7.4 us (5%)
  other arithmetic  5.3 us (4%)
    all_gather x1, waiting for transfers between devices, body(): whole = lax.all_gather(coefficients, 'irrep', axis=1, tiled=True)  64.7 us
    gather x2, local copies, waits for them, and re-layouts, body(): jnp.take(masked, shell_batch_functions, axis=0).reshape(NAO, NIRR, VIR)  21.9 us
    dot_general x1, matrix products, body(): jnp.dot(gathered.reshape(local_pair_list * NAO, NAO), masked, preferred_e...  10.5 us
    another operation x1, local copies, waits for them, and re-layouts, one_pair(): half_three = half.reshape(half.shape[0], NIRR, VIR)  7.81 us
    all_to_all x1, starting transfers between devices, body(): lax.all_to_all(blocks.reshape(pairs_here, batch_rows, NAO), 'pair', split...  7.4 us
    dot_general x1, matrix products, one_pair(): jnp.einsum('ytq,ytj->tqj', third_row_group, selected_option, preferred_el...  7.1 us
    gather x2, local copies, waits for them, and re-layouts, one_pair(): selected_option = jnp.take(half_three, partner_irrep, axis=1)  5.74 us
    select_n x1, other arithmetic, mask_columns(): return jnp.where(live[None, :], whole, jnp.zeros_like(whole))  5.15 us
  transfers between devices with their start and end apart: 2, of which 1 were waited for; matrix products, arithmetic and copies ran while one was open for 19% of the time, Pallas kernels for 0%

commit v1 on v0

v1 whole, which is shorter than its diff:
```python
import functools

import jax
import jax.numpy as jnp
from jax import lax
from jax.experimental import pallas as pl
from jax.experimental.pallas import tpu as pltpu
from jax.sharding import PartitionSpec as P

VIR = 256
INNER = 4
MESH = pl.DeviceIdType.MESH


def kernel(
    n, ni, blocks, coef, batch, sym, out,
    recv, c_all, perm, rows_t, half,
    b_send, b_recv, c_send, c_recv, f_send, f_recv, own_sem, c_own_sem,
):
    me = lax.axis_index("pair")
    qi = lax.axis_index("irrep")
    rows = blocks.shape[2]
    nao = coef.shape[0]
    per = coef.shape[1] // VIR
    irr = ni * per
    levels = n // INNER
    h = levels // 2
    lev, inner, core = me // INNER, me % INNER, me % 2
    sibling = me + 1 - 2 * core
    span = INNER * rows

    def level_at(step):
        if step < h:
            return (lev // h) * h + (lev % h + step) % h
        return ((lev // h + 1) % 2) * h + (lev % h + step) % h

    barrier = pltpu.get_barrier_semaphore()
    for k in range(1, n):
        pl.semaphore_signal(barrier, inc=1, device_id=((me + k) % n, qi), device_id_type=MESH)
    for d in range(1, ni):
        pl.semaphore_signal(barrier, inc=1, device_id=(me, (qi + d) % ni), device_id_type=MESH)
    own = pltpu.make_async_copy(blocks.at[me, 0], recv.at[me], own_sem)
    own.start()
    c_own = []
    for j in range(per):
        cp = pltpu.make_async_copy(
            coef.at[:, pl.ds(j * VIR, VIR)], c_all.at[qi * per + j], c_own_sem.at[j]
        )
        cp.start()
        c_own.append(cp)
    pl.semaphore_wait(barrier, n - 1 + ni - 1)

    part = pl.ds(pl.multiple_of(core * (nao // 2), nao // 2), nao // 2)
    other = pl.ds(pl.multiple_of((1 - core) * (nao // 2), nao // 2), nao // 2)
    c_copies = []
    for d in range(1, ni):
        for j in range(per):
            t = (d - 1) * per + j
            cp = pltpu.make_async_remote_copy(
                src_ref=coef.at[part, pl.ds(j * VIR, VIR)],
                dst_ref=c_all.at[qi * per + j, part],
                send_sem=c_send.at[t],
                recv_sem=c_recv.at[t],
                device_id=(me, (qi + d) % ni),
                device_id_type=MESH,
            )
            cp.start()
            c_copies.append(cp)

    b_copies = []
    for step in list(range(h, levels)) + list(range(h - 1, -1, -1)):
        for i in range(INNER):
            if step == 0 and i == 0:
                continue
            to = level_at(step) * INNER + (inner + i) % INNER
            cp = pltpu.make_async_remote_copy(
                src_ref=blocks.at[to, 0],
                dst_ref=recv.at[me],
                send_sem=b_send.at[to],
                recv_sem=b_recv.at[me],
                device_id=(to, qi),
                device_id_type=MESH,
            )
            cp.start()
            b_copies.append(cp)

    strip = 128

    @pl.loop(0, nao // strip)
    def _(k):
        base = pl.multiple_of(k * strip, strip)
        nu = lax.broadcasted_iota(jnp.int32, (strip, nao), 0) + base
        perm[pl.ds(base, strip), :] = jnp.where(nu == batch[...], 1.0, 0.0).astype(jnp.bfloat16)

    f_copies = []
    for d in range(1, ni):
        for j in range(per):
            t = (d - 1) * per + j
            slab = ((qi + ni - d) % ni) * per + j
            c_copies[t].wait_recv()
            cp = pltpu.make_async_remote_copy(
                src_ref=c_all.at[slab, part],
                dst_ref=c_all.at[slab, part],
                send_sem=f_send.at[t],
                recv_sem=f_recv.at[t],
                device_id=(sibling, qi),
                device_id_type=MESH,
            )
            cp.start()
            f_copies.append((cp, slab, t))
    for cp in c_own:
        cp.wait()
    for cp, slab, t in f_copies:
        cp.wait_recv()

    @pl.loop(0, irr)
    def _(r):
        rows_t[r] = lax.dot_general(
            c_all[r], perm[...], (((0,), (0,)), ((), ())), preferred_element_type=jnp.float32
        ).astype(jnp.bfloat16)

    own.wait()
    for step in range(levels):
        lv = level_at(step)
        for i in range(INNER):
            if step == 0 and i == 0:
                continue
            src = lv * INNER + (inner + i) % INNER
            pltpu.make_async_remote_copy(
                src_ref=blocks.at[src, 0],
                dst_ref=recv.at[src],
                send_sem=b_send.at[src],
                recv_sem=b_recv.at[src],
                device_id=(src, qi),
                device_id_type=MESH,
            ).wait_recv()
        base = pl.multiple_of(lv * span, span)

        @pl.loop(0, irr)
        def _(c):
            x = recv[pl.ds(lv * INNER, INNER)].reshape(span, nao)
            half[c, pl.ds(base, span), :] = jnp.dot(
                x, c_all[c], preferred_element_type=jnp.float32
            ).astype(jnp.bfloat16)

    s = sym[0, 0]

    @pl.loop(0, irr)
    def _(r):
        out[r] = jnp.dot(
            rows_t[r], half[jnp.bitwise_xor(r, s)], preferred_element_type=jnp.float32
        )

    for cp in c_copies + b_copies:
        cp.wait_send()
    for cp, _, _ in f_copies:
        cp.wait_send()


def body(n, ni, blocks, coefficients, shell_batch_functions, irrep_counts, pair_symmetry):
    rows, nao = blocks.shape[2], blocks.shape[3]
    per = coefficients.shape[1] // VIR
    irr = per * ni
    remote = max(1, (ni - 1) * per)
    dma = pltpu.SemaphoreType.DMA
    full = pl.pallas_call(
        functools.partial(kernel, n, ni),
        out_shape=jax.ShapeDtypeStruct((irr, VIR, VIR), jnp.float32),
        in_specs=[
            pl.BlockSpec(memory_space=pl.ANY),
            pl.BlockSpec(memory_space=pl.ANY),
            pl.BlockSpec(memory_space=pltpu.VMEM),
            pl.BlockSpec(memory_space=pltpu.SMEM),
        ],
        out_specs=pl.BlockSpec(memory_space=pltpu.VMEM),
        scratch_shapes=[
            pltpu.VMEM((n, rows, nao), jnp.bfloat16),
            pltpu.VMEM((irr, nao, VIR), jnp.bfloat16),
            pltpu.VMEM((nao, nao), jnp.bfloat16),
            pltpu.VMEM((irr, VIR, nao), jnp.bfloat16),
            pltpu.VMEM((irr, nao, VIR), jnp.bfloat16),
            dma((n,)), dma((n,)), dma((remote,)), dma((remote,)),
            dma((remote,)), dma((remote,)), dma, dma((per,)),
        ],
        compiler_params=pltpu.CompilerParams(
            collective_id=0, has_side_effects=True, vmem_limit_bytes=56 * 2**20
        ),
    )(blocks, coefficients, shell_batch_functions.reshape(1, nao), pair_symmetry)
    label = jnp.arange(irr, dtype=jnp.int32)
    left = irrep_counts
    right = jnp.take(irrep_counts, jnp.bitwise_xor(label, pair_symmetry[0, 0]))
    col = jnp.arange(VIR, dtype=jnp.int32)
    live = (col[None, :, None] < left[:, None, None]) & (col[None, None, :] < right[:, None, None])
    return jnp.where(live, full, 0.0)[None, None]


def solution(mesh):
    in_specs = (P(None, "irrep", "pair", None), P(None, "irrep"), P(), P(), P("pair", "irrep"))
    out_specs = P("pair", "irrep", None, None, None)
    return jax.shard_map(
        functools.partial(body, mesh.shape["pair"], mesh.shape["irrep"]),
        mesh=mesh, in_specs=in_specs, out_specs=out_specs, check_vma=False,
    )
```

time: 146 us -> 89.7 us (0.61)
  the two profiles are of different devices: /device:TPU:0 before, /device:TPU:19 now
where the time goes in v1:
time: 89.7 us; the launch traced here: 89.3 us
  Pallas kernels  83.8 us (93%)
  other arithmetic  2.86 us (3%)
  local copies, waits for them, and re-layouts  1.94 us (2%)
    pallas_call x1, Pallas kernels, body(): pl.pallas_call(functools.partial(kernel, n, ni), out_shape=jax.ShapeDtype...  83.8 us
    broadcast_in_dim x1, other arithmetic, body(): return jnp.where(live, full, 0.0)[None, None]  2.76 us

profile of v1, /device:TPU:19, one launch (start us, length us, event | category | flops | bytes accessed | tf_op | source)
XLA Modules:
  0.0 89.3 jit_solution(8382616039476969812)
XLA Ops:
  0.0 1.3 %reshape.84.batch = s32[1,1280]{1,0:T(1,128)} reshape(s32[1280]{0:T(1024)} %param.7) | data formatting | bytes 10240 | tf_op jit(solution)/shard_map/reshape | solution.py:188
  1.9 0.0 copy-start
  2.0 83.8 %shard_map.55 = f32[8,256,256]{2,1,0:T(8,128)} custom-call(bf16[16,1,80,1280]{3,2,1,0:T(8,128)(2,1)} %blocks.1, bf16[1280,1024]{1,0:T(8,128)(2,1)} %coef.1, s32[1,1280]{1,0:T(1,128)} %reshape.84.batch, s32[1,1]{1,0:T(1,128)} %copy.6.sym), custom_call_target="tpu_custom_call" | custom-call | tf_op jit(solution)/shard_map/pallas_call | solution.py:166
  85.8 0.0 copy-done
  85.8 0.6 gather_fusion
  86.5 0.1 iota_compare_fusion
  86.6 2.8 %select_bitcast_fusion = f32[1,1,8,256,256]{4,3,2,1,0:T(8,128)} fusion(f32[8,256,256]{2,1,0:T(8,128)} %shard_map.55, pred[8,256]{1,0:T(8,128)(4,1)S(1)} %get-tuple-element.5, pred[8,256]{1,0:T(8,128)(4,1)S(1)} %get-tuple-element.6), kind=kLoop, calls=%fused_computation.1 | loop fusion | flops 1048576 | bytes 4198400 | tf_op jit(solution)/shard_map/broadcast_in_dim | solution.py:194
  (3 shorter events, 0.0 us)
Async XLA Ops:
  1.9 83.9 %copy-start = (s32[8]{0:T(128)S(1)}, s32[8]{0:T(128)}, u32[]{:S(2)}) copy-start(s32[8]{0:T(128)} %param.8) | copy-start | bytes 100

commit v2 on v1

--- a/solution.py
+++ b/solution.py
@@ -13,9 +13,11 @@
 
 
 def kernel(
-    n, ni, blocks, coef, batch, sym, out,
+    n, ni, blocks, coef, batch, sym, sym_v, out,
     recv, c_all, perm, rows_t, half,
     b_send, b_recv, c_send, c_recv, f_send, f_recv, own_sem, c_own_sem,
+    rel_rows, rel_half, p_out, p_in, sym_in, sym_s,
+    a_send, a_recv, p_send, p_recv, s_send, s_recv, a_own_sem, s_own_sem,
 ):
     me = lax.axis_index("pair")
     qi = lax.axis_index("irrep")
@@ -28,6 +30,13 @@
     lev, inner, core = me // INNER, me % INNER, me % 2
     sibling = me + 1 - 2 * core
     span = INNER * rows
+    relay = levels == 4
+    hf = lev // h
+    half_rows = h * span
+    half_base = pl.multiple_of(hf * half_rows, half_rows)
+    is_mid = ((lev + 1) // 2) % 2 == 1
+    is_end = ((lev + 1) // 2) % 2 == 0
+    own_mid, far_mid, far_end = 1 + hf, 2 - hf, 3 * (1 - hf)
 
     def level_at(step):
         if step < h:
@@ -67,12 +76,49 @@
             cp.start()
             c_copies.append(cp)
 
+    def relay_copy(i, at):
+        to = own_mid * INNER + i
+        return pltpu.make_async_remote_copy(
+            src_ref=blocks.at[far_end * INNER + i, 0],
+            dst_ref=rel_rows.at[at],
+            send_sem=a_send.at[i],
+            recv_sem=a_recv.at[at],
+            device_id=(to, qi),
+            device_id_type=MESH,
+        )
+
+    my_slot = me - hf * h * INNER
+    a_local = pltpu.make_async_copy(
+        blocks.at[far_end * INNER + inner, 0], rel_rows.at[my_slot], a_own_sem
+    )
+    s_copy = pltpu.make_async_remote_copy(
+        src_ref=sym_v, dst_ref=sym_in, send_sem=s_send, recv_sem=s_recv,
+        device_id=(far_mid * INNER + inner, qi), device_id_type=MESH,
+    )
+    if relay:
+        for k in range(1, INNER):
+            relay_copy((inner + k) % INNER, my_slot).start()
+
+        @pl.when(is_mid)
+        def _():
+            a_local.start()
+
+        @pl.when(is_end)
+        def _():
+            s_copy.start()
+            relay_copy(inner, my_slot).start()
+
+        order = [None] + list(range(h - 1, -1, -1))
+    else:
+        order = list(range(h, levels)) + list(range(h - 1, -1, -1))
+
     b_copies = []
-    for step in list(range(h, levels)) + list(range(h - 1, -1, -1)):
+    for step in order:
         for i in range(INNER):
             if step == 0 and i == 0:
                 continue
-            to = level_at(step) * INNER + (inner + i) % INNER
+            target = far_mid if step is None else level_at(step)
+            to = target * INNER + (inner + i) % INNER
             cp = pltpu.make_async_remote_copy(
                 src_ref=blocks.at[to, 0],
                 dst_ref=recv.at[me],
@@ -91,6 +137,18 @@
         base = pl.multiple_of(k * strip, strip)
         nu = lax.broadcasted_iota(jnp.int32, (strip, nao), 0) + base
         perm[pl.ds(base, strip), :] = jnp.where(nu == batch[...], 1.0, 0.0).astype(jnp.bfloat16)
+
+    def make_rows_t(r):
+        rows_t[r] = lax.dot_general(
+            c_all[r], perm[...], (((0,), (0,)), ((), ())), preferred_element_type=jnp.float32
+        ).astype(jnp.bfloat16)
+
+    for cp in c_own:
+        cp.wait()
+
+    @pl.loop(0, per)
+    def _(j):
+        make_rows_t(qi * per + j)
 
     f_copies = []
     for d in range(1, ni):
@@ -108,19 +166,58 @@
             )
             cp.start()
             f_copies.append((cp, slab, t))
-    for cp in c_own:
-        cp.wait()
-    for cp, slab, t in f_copies:
-        cp.wait_recv()
-
-    @pl.loop(0, irr)
-    def _(r):
-        rows_t[r] = lax.dot_general(
-            c_all[r], perm[...], (((0,), (0,)), ((), ())), preferred_element_type=jnp.float32
-        ).astype(jnp.bfloat16)
+            if t >= 1:
+                prev, prev_slab, _ = f_copies[t - 1]
+                prev.wait_recv()
+                make_rows_t(prev_slab)
+    last, last_slab, _ = f_copies[-1]
+    last.wait_recv()
+    make_rows_t(last_slab)
+
+    def p_copy(r):
+        return pltpu.make_async_remote_copy(
+            src_ref=p_out.at[r], dst_ref=p_in.at[r],
+            send_sem=p_send.at[r], recv_sem=p_recv.at[r],
+            device_id=(far_end * INNER + inner, qi), device_id_type=MESH,
+        )
+
+    if relay:
+
+        @pl.when(is_mid)
+        def _():
+            s_copy.wait_recv()
+            to_smem = pltpu.make_async_copy(sym_in, sym_s, s_own_sem)
+            to_smem.start()
+            a_local.wait()
+            for step in range(h):
+                for i in range(INNER):
+                    if step == 0 and i == 0:
+                        continue
+                    at = ((lev % h + step) % h) * INNER + (inner + i) % INNER
+                    relay_copy(inner, at).wait_recv()
+            to_smem.wait()
+
+            @pl.loop(0, irr)
+            def _(c):
+                x = rel_rows[...].reshape(half_rows, nao)
+                rel_half[c] = jnp.dot(
+                    x, c_all[c], preferred_element_type=jnp.float32
+                ).astype(jnp.bfloat16)
+
+            their = sym_s[0, 0]
+
+            @pl.loop(0, irr)
+            def _(r):
+                p_out[r] = jnp.dot(
+                    rows_t[r, :, pl.ds(half_base, half_rows)],
+                    rel_half[jnp.bitwise_xor(r, their)],
+                    preferred_element_type=jnp.float32,
+                ).astype(jnp.bfloat16)
+                p_copy(r).start()
 
     own.wait()
-    for step in range(levels):
+
+    def do_level(step):
         lv = level_at(step)
         for i in range(INNER):
             if step == 0 and i == 0:
@@ -145,11 +242,51 @@
 
     s = sym[0, 0]
 
-    @pl.loop(0, irr)
-    def _(r):
-        out[r] = jnp.dot(
-            rows_t[r], half[jnp.bitwise_xor(r, s)], preferred_element_type=jnp.float32
-        )
+    def finish_all():
+        @pl.loop(0, irr)
+        def _(r):
+            out[r] = jnp.dot(
+                rows_t[r], half[jnp.bitwise_xor(r, s)], preferred_element_type=jnp.float32
+            )
+
+    if relay:
+        for step in range(h):
+            do_level(step)
+
+        @pl.when(is_mid)
+        def _():
+            for step in range(h, levels):
+                do_level(step)
+            finish_all()
+            for k in range(1, INNER):
+                relay_copy((inner + k) % INNER, my_slot).wait_send()
+
+            @pl.loop(0, irr)
+            def _(r):
+                p_copy(r).wait_send()
+
+        @pl.when(is_end)
+        def _():
+            @pl.loop(0, irr)
+            def _(r):
+                out[r] = jnp.dot(
+                    rows_t[r, :, pl.ds(half_base, half_rows)],
+                    half[jnp.bitwise_xor(r, s), pl.ds(half_base, half_rows), :],
+                    preferred_element_type=jnp.float32,
+                )
+
+            @pl.loop(0, irr)
+            def _(r):
+                p_copy(r).wait_recv()
+                out[r] = out[r] + p_in[r].astype(jnp.float32)
+
+            for k in range(INNER):
+                relay_copy((inner + k) % INNER, my_slot).wait_send()
+            s_copy.wait_send()
+    else:
+        for step in range(levels):
+            do_level(step)
+        finish_all()
 
     for cp in c_copies + b_copies:
         cp.wait_send()
@@ -171,6 +308,7 @@
             pl.BlockSpec(memory_space=pl.ANY),
             pl.BlockSpec(memory_space=pltpu.VMEM),
             pl.BlockSpec(memory_space=pltpu.SMEM),
+            pl.BlockSpec(memory_space=pltpu.VMEM),
         ],
         out_specs=pl.BlockSpec(memory_space=pltpu.VMEM),
         scratch_shapes=[
@@ -181,11 +319,20 @@
             pltpu.VMEM((irr, nao, VIR), jnp.bfloat16),
             dma((n,)), dma((n,)), dma((remote,)), dma((remote,)),
             dma((remote,)), dma((remote,)), dma, dma((per,)),
+            pltpu.VMEM((n // 2, rows, nao), jnp.bfloat16),
+            pltpu.VMEM((irr, nao // 2, VIR), jnp.bfloat16),
+            pltpu.VMEM((irr, VIR, VIR), jnp.bfloat16),
+            pltpu.VMEM((irr, VIR, VIR), jnp.bfloat16),
+            pltpu.VMEM((8, 128), jnp.int32),
+            pltpu.SMEM((8, 128), jnp.int32),
+            dma((INNER,)), dma((n // 2,)), dma((irr,)), dma((irr,)),
+            dma, dma, dma, dma,
         ],
         compiler_params=pltpu.CompilerParams(
             collective_id=0, has_side_effects=True, vmem_limit_bytes=56 * 2**20
         ),
-    )(blocks, coefficients, shell_batch_functions.reshape(1, nao), pair_symmetry)
+    )(blocks, coefficients, shell_batch_functions.reshape(1, nao), pair_symmetry,
+      jnp.broadcast_to(pair_symmetry, (8, 128)))
     label = jnp.arange(irr, dtype=jnp.int32)
     left = irrep_counts
     right = jnp.take(irrep_counts, jnp.bitwise_xor(label, pair_symmetry[0, 0]))

time: 89.7 us -> 82.1 us (0.915)
  the two profiles are of different devices: /device:TPU:19 before, /device:TPU:9 now
where the time goes in v2:
time: 82.1 us; the launch traced here: 81.9 us
  Pallas kernels  75.8 us (92%)
  other arithmetic  2.86 us (3%)
  local copies, waits for them, and re-layouts  2.53 us (3%)
    pallas_call x1, Pallas kernels, body(): pl.pallas_call(functools.partial(kernel, n, ni), out_shape=jax.ShapeDtype...  75.8 us
    broadcast_in_dim x1, other arithmetic, body(): return jnp.where(live, full, 0.0)[None, None]  2.76 us

profile of v2, /device:TPU:9, one launch (start us, length us, event | category | flops | bytes accessed | tf_op | source)
XLA Modules:
  0.0 81.9 jit_solution(3413131797149694759)
XLA Ops:
  0.0 1.3 %reshape.84.batch = s32[1,1280]{1,0:T(1,128)} reshape(s32[1280]{0:T(1024)} %param.7) | data formatting | bytes 10240 | tf_op jit(solution)/shard_map/reshape | solution.py:334
  1.9 0.6 broadcast_in_dim.9.sym_v
  2.5 0.0 copy-start
  2.5 75.8 %shard_map.55 = f32[8,256,256]{2,1,0:T(8,128)} custom-call(bf16[16,1,80,1280]{3,2,1,0:T(8,128)(2,1)} %blocks.1, bf16[1280,1024]{1,0:T(8,128)(2,1)} %coef.1, s32[1,1280]{1,0:T(1,128)} %reshape.84.batch, s32[1,1]{1,0:T(1,128)} %copy.6.sym, s32[8,128]{1,0:T(8,128)} %broadcast_in_dim.9.sym_v), custom_call_target="tpu_custom_call" | custom-call | tf_op jit(solution)/shard_map/pallas_call | solution.py:303
  78.4 0.0 copy-done
  78.4 0.6 gather_fusion
  79.1 0.1 iota_compare_fusion
  79.1 2.8 %select_bitcast_fusion = f32[1,1,8,256,256]{4,3,2,1,0:T(8,128)} fusion(f32[8,256,256]{2,1,0:T(8,128)} %shard_map.55, pred[8,256]{1,0:T(8,128)(4,1)S(1)} %get-tuple-element.5, pred[8,256]{1,0:T(8,128)(4,1)S(1)} %get-tuple-element.6), kind=kLoop, calls=%fused_computation.1 | loop fusion | flops 1048576 | bytes 4198400 | tf_op jit(solution)/shard_map/broadcast_in_dim | solution.py:341
  (3 shorter events, 0.0 us)
Async XLA Ops:
  2.5 75.9 %copy-start = (s32[8]{0:T(128)S(1)}, s32[8]{0:T(128)}, u32[]{:S(2)}) copy-start(s32[8]{0:T(128)} %param.8) | copy-start | bytes 100

commit v3 on v2

--- a/solution.py
+++ b/solution.py
@@ -13,10 +13,10 @@
 
 
 def kernel(
-    n, ni, blocks, coef, batch, sym, sym_v, out,
+    n, ni, blocks, coef, batch, sym, out,
     recv, c_all, perm, rows_t, half,
     b_send, b_recv, c_send, c_recv, f_send, f_recv, own_sem, c_own_sem,
-    rel_rows, rel_half, p_out, p_in, sym_in, sym_s,
+    rel_rows, rel_half, p_out, p_in, sym_v, sym_in, sym_s,
     a_send, a_recv, p_send, p_recv, s_send, s_recv, a_own_sem, s_own_sem,
 ):
     me = lax.axis_index("pair")
@@ -105,6 +105,7 @@
 
         @pl.when(is_end)
         def _():
+            sym_v[...] = jnp.full((8, 128), sym[0, 0], jnp.int32)
             s_copy.start()
             relay_copy(inner, my_slot).start()
 
@@ -113,6 +114,7 @@
         order = list(range(h, levels)) + list(range(h - 1, -1, -1))
 
     b_copies = []
+    near_copies = []
     for step in order:
         for i in range(INNER):
             if step == 0 and i == 0:
@@ -127,8 +129,19 @@
                 device_id=(to, qi),
                 device_id_type=MESH,
             )
+            (b_copies if step is None or step >= h else near_copies).append(cp)
+
+    def start(copies):
+        for cp in copies:
             cp.start()
-            b_copies.append(cp)
+
+    if relay:
+
+        @pl.when(is_mid)
+        def _():
+            start(b_copies + near_copies)
+    else:
+        start(b_copies + near_copies)
 
     strip = 128
 
@@ -136,7 +149,7 @@
     def _(k):
         base = pl.multiple_of(k * strip, strip)
         nu = lax.broadcasted_iota(jnp.int32, (strip, nao), 0) + base
-        perm[pl.ds(base, strip), :] = jnp.where(nu == batch[...], 1.0, 0.0).astype(jnp.bfloat16)
+        perm[pl.ds(base, strip), :] = jnp.where(nu == batch[...][None, :], 1.0, 0.0).astype(jnp.bfloat16)
 
     def make_rows_t(r):
         rows_t[r] = lax.dot_general(
@@ -149,6 +162,33 @@
     @pl.loop(0, per)
     def _(j):
         make_rows_t(qi * per + j)
+
+    if relay:
+
+        @pl.when(is_end)
+        def _():
+            start(b_copies)
+
+    def relay_transform(slab):
+        x = rel_rows[...].reshape(half_rows, nao)
+        rel_half[slab] = jnp.dot(
+            x, c_all[slab], preferred_element_type=jnp.float32
+        ).astype(jnp.bfloat16)
+
+    early = (ni - 1) * per - 2
+
+    def relay_early():
+        a_local.wait()
+        for step in range(h):
+            for i in range(INNER):
+                if step == 0 and i == 0:
+                    continue
+                at = ((lev % h + step) % h) * INNER + (inner + i) % INNER
+                relay_copy(inner, at).wait_recv()
+
+        @pl.loop(0, per)
+        def _(j):
+            relay_transform(qi * per + j)
 
     f_copies = []
     for d in range(1, ni):
@@ -170,6 +210,14 @@
                 prev, prev_slab, _ = f_copies[t - 1]
                 prev.wait_recv()
                 make_rows_t(prev_slab)
+            if relay and t == early:
+                pl.when(is_mid)(relay_early)
+    if relay:
+
+        @pl.when(is_end)
+        def _():
+            start(near_copies)
+
     last, last_slab, _ = f_copies[-1]
     last.wait_recv()
     make_rows_t(last_slab)
@@ -188,21 +236,11 @@
             s_copy.wait_recv()
             to_smem = pltpu.make_async_copy(sym_in, sym_s, s_own_sem)
             to_smem.start()
-            a_local.wait()
-            for step in range(h):
-                for i in range(INNER):
-                    if step == 0 and i == 0:
-                        continue
-                    at = ((lev % h + step) % h) * INNER + (inner + i) % INNER
-                    relay_copy(inner, at).wait_recv()
             to_smem.wait()
 
-            @pl.loop(0, irr)
-            def _(c):
-                x = rel_rows[...].reshape(half_rows, nao)
-                rel_half[c] = jnp.dot(
-                    x, c_all[c], preferred_element_type=jnp.float32
-                ).astype(jnp.bfloat16)
+            @pl.loop(per, irr)
+            def _(k):
+                relay_transform((qi * per + k) % irr)
 
             their = sym_s[0, 0]
 
@@ -250,14 +288,34 @@
             )
 
     if relay:
-        for step in range(h):
-            do_level(step)
+        other_base = pl.multiple_of((1 - hf) * half_rows, half_rows)
+
+        def folded(r, base):
+            return jnp.dot(
+                rows_t[r, :, pl.ds(base, half_rows)],
+                half[jnp.bitwise_xor(r, s), pl.ds(base, half_rows), :],
+                preferred_element_type=jnp.float32,
+            )
+
+        do_level(0)
 
         @pl.when(is_mid)
         def _():
             for step in range(h, levels):
                 do_level(step)
-            finish_all()
+
+            @pl.loop(0, irr)
+            def _(r):
+                out[r] = folded(r, other_base)
+
+        do_level(1)
+
+        @pl.when(is_mid)
+        def _():
+            @pl.loop(0, irr)
+            def _(r):
+                out[r] = out[r] + folded(r, half_base)
+
             for k in range(1, INNER):
                 relay_copy((inner + k) % INNER, my_slot).wait_send()
 
@@ -269,11 +327,7 @@
         def _():
             @pl.loop(0, irr)
             def _(r):
-                out[r] = jnp.dot(
-                    rows_t[r, :, pl.ds(half_base, half_rows)],
-                    half[jnp.bitwise_xor(r, s), pl.ds(half_base, half_rows), :],
-                    preferred_element_type=jnp.float32,
-                )
+                out[r] = folded(r, half_base)
 
             @pl.loop(0, irr)
             def _(r):
@@ -288,7 +342,7 @@
             do_level(step)
         finish_all()
 
-    for cp in c_copies + b_copies:
+    for cp in c_copies + b_copies + near_copies:
         cp.wait_send()
     for cp, _, _ in f_copies:
         cp.wait_send()
@@ -308,7 +362,6 @@
             pl.BlockSpec(memory_space=pl.ANY),
             pl.BlockSpec(memory_space=pltpu.VMEM),
             pl.BlockSpec(memory_space=pltpu.SMEM),
-            pl.BlockSpec(memory_space=pltpu.VMEM),
         ],
         out_specs=pl.BlockSpec(memory_space=pltpu.VMEM),
         scratch_shapes=[
@@ -324,6 +377,7 @@
             pltpu.VMEM((irr, VIR, VIR), jnp.bfloat16),
             pltpu.VMEM((irr, VIR, VIR), jnp.bfloat16),
             pltpu.VMEM((8, 128), jnp.int32),
+            pltpu.VMEM((8, 128), jnp.int32),
             pltpu.SMEM((8, 128), jnp.int32),
             dma((INNER,)), dma((n // 2,)), dma((irr,)), dma((irr,)),
             dma, dma, dma, dma,
@@ -331,11 +385,11 @@
         compiler_params=pltpu.CompilerParams(
             collective_id=0, has_side_effects=True, vmem_limit_bytes=56 * 2**20
         ),
-    )(blocks, coefficients, shell_batch_functions.reshape(1, nao), pair_symmetry,
-      jnp.broadcast_to(pair_symmetry, (8, 128)))
+    )(blocks, coefficients, shell_batch_functions, pair_symmetry)
     label = jnp.arange(irr, dtype=jnp.int32)
     left = irrep_counts
-    right = jnp.take(irrep_counts, jnp.bitwise_xor(label, pair_symmetry[0, 0]))
+    partner = jnp.bitwise_xor(label, pair_symmetry[0, 0])
+    right = jnp.sum(jnp.where(partner[:, None] == label[None, :], irrep_counts[None, :], 0), axis=1)
     col = jnp.arange(VIR, dtype=jnp.int32)
     live = (col[None, :, None] < left[:, None, None]) & (col[None, None, :] < right[:, None, None])
     return jnp.where(live, full, 0.0)[None, None]

time: 82.1 us -> 79.8 us (0.972)
  the two profiles are of different devices: /device:TPU:9 before, /device:TPU:19 now
where the time goes in v3:
time: 79.8 us; the launch traced here: 79.6 us
  Pallas kernels  74.6 us (93%)
  other arithmetic  4.33 us (5%)
    pallas_call x1, Pallas kernels, body(): pl.pallas_call(functools.partial(kernel, n, ni), out_shape=jax.ShapeDtype...  74.6 us
    broadcast_in_dim x1, other arithmetic, body(): return jnp.where(live, full, 0.0)[None, None]  2.76 us

profile of v3, /device:TPU:19, one launch (start us, length us, event | category | flops | bytes accessed | tf_op | source)
XLA Modules:
  0.0 79.6 jit_solution(10825673175735817775)
XLA Ops:
  0.7 0.8 %select_reduce_fusion = s32[8]{0:T(128)S(1)} fusion(s32[8]{0:T(128)} %param.8, s32[8]{0:T(128)S(1)} %iota_xor_fusion), kind=kLoop, calls=%fused_computation.3 | loop fusion | flops 184 | bytes 96 | tf_op jit(solution)/shard_map/reduce_sum | solution.py:392
  1.5 0.7 iota_compare_fusion
  2.2 74.6 %shard_map.55 = f32[8,256,256]{2,1,0:T(8,128)} custom-call(bf16[16,1,80,1280]{3,2,1,0:T(8,128)(2,1)} %blocks.1, bf16[1280,1024]{1,0:T(8,128)(2,1)} %coef.1, s32[1280]{0:T(1024)} %batch.1, s32[1,1]{1,0:T(1,128)} %copy.6.sym), custom_call_target="tpu_custom_call" | custom-call | tf_op jit(solution)/shard_map/pallas_call | solution.py:357
  76.8 2.8 %select_bitcast_fusion = f32[1,1,8,256,256]{4,3,2,1,0:T(8,128)} fusion(f32[8,256,256]{2,1,0:T(8,128)} %shard_map.55, pred[8,256]{1,0:T(8,128)(4,1)S(1)} %get-tuple-element.5, pred[8,256]{1,0:T(8,128)(4,1)S(1)} %get-tuple-element.6), kind=kLoop, calls=%fused_computation | loop fusion | flops 1048576 | bytes 4198400 | tf_op jit(solution)/shard_map/broadcast_in_dim | solution.py:395
  (1 shorter events, 0.0 us)

commit v4 on v3

--- a/solution.py
+++ b/solution.py
@@ -13,7 +13,7 @@
 
 
 def kernel(
-    n, ni, blocks, coef, batch, sym, out,
+    n, ni, blocks, coef, batch, sym, counts, out,
     recv, c_all, perm, rows_t, half,
     b_send, b_recv, c_send, c_recv, f_send, f_recv, own_sem, c_own_sem,
     rel_rows, rel_half, p_out, p_in, sym_v, sym_in, sym_s,
@@ -280,12 +280,18 @@
 
     s = sym[0, 0]
 
+    def masked(r, whole):
+        a = lax.broadcasted_iota(jnp.int32, (VIR, VIR), 0)
+        b = lax.broadcasted_iota(jnp.int32, (VIR, VIR), 1)
+        live = (a < counts[r]) & (b < counts[jnp.bitwise_xor(r, s)])
+        return jnp.where(live, whole, 0.0)
+
     def finish_all():
         @pl.loop(0, irr)
         def _(r):
-            out[r] = jnp.dot(
+            out[r] = masked(r, jnp.dot(
                 rows_t[r], half[jnp.bitwise_xor(r, s)], preferred_element_type=jnp.float32
-            )
+            ))
 
     if relay:
         other_base = pl.multiple_of((1 - hf) * half_rows, half_rows)
@@ -314,7 +320,7 @@
         def _():
             @pl.loop(0, irr)
             def _(r):
-                out[r] = out[r] + folded(r, half_base)
+                out[r] = masked(r, out[r] + folded(r, half_base))
 
             for k in range(1, INNER):
                 relay_copy((inner + k) % INNER, my_slot).wait_send()
@@ -332,7 +338,7 @@
             @pl.loop(0, irr)
             def _(r):
                 p_copy(r).wait_recv()
-                out[r] = out[r] + p_in[r].astype(jnp.float32)
+                out[r] = masked(r, out[r] + p_in[r].astype(jnp.float32))
 
             for k in range(INNER):
                 relay_copy((inner + k) % INNER, my_slot).wait_send()
@@ -361,6 +367,7 @@
             pl.BlockSpec(memory_space=pl.ANY),
             pl.BlockSpec(memory_space=pl.ANY),
             pl.BlockSpec(memory_space=pltpu.VMEM),
+            pl.BlockSpec(memory_space=pltpu.SMEM),
             pl.BlockSpec(memory_space=pltpu.SMEM),
         ],
         out_specs=pl.BlockSpec(memory_space=pltpu.VMEM),
@@ -385,14 +392,8 @@
         compiler_params=pltpu.CompilerParams(
             collective_id=0, has_side_effects=True, vmem_limit_bytes=56 * 2**20
         ),
-    )(blocks, coefficients, shell_batch_functions, pair_symmetry)
-    label = jnp.arange(irr, dtype=jnp.int32)
-    left = irrep_counts
-    partner = jnp.bitwise_xor(label, pair_symmetry[0, 0])
-    right = jnp.sum(jnp.where(partner[:, None] == label[None, :], irrep_counts[None, :], 0), axis=1)
-    col = jnp.arange(VIR, dtype=jnp.int32)
-    live = (col[None, :, None] < left[:, None, None]) & (col[None, None, :] < right[:, None, None])
-    return jnp.where(live, full, 0.0)[None, None]
+    )(blocks, coefficients, shell_batch_functions, pair_symmetry, irrep_counts)
+    return full[None, None]
 
 
 def solution(mesh):

time: 79.8 us -> 78.8 us (0.987)
  other arithmetic: 4.33 us -> 0 us
  local copies, waits for them, and re-layouts: 0 us -> 3.05 us
    unnamed x0 -> x1, local copies, waits for them, and re-layouts: none -> 3.05 us
    broadcast_in_dim x1 -> x0, other arithmetic: 2.76 us -> none  [body(): return jnp.where(live, full, 0.0)[None, None]]
    reduce_sum x1 -> x0, other arithmetic: 0.84 us -> none  [body(): jnp.sum(jnp.where(partner[:, None] == label[None, :], irrep_counts[None,...]
where the time goes in v4:
time: 78.8 us; the launch traced here: 78.6 us
  Pallas kernels  74.9 us (95%)
  local copies, waits for them, and re-layouts  3.05 us (4%)
    pallas_call x1, Pallas kernels, body(): pl.pallas_call(functools.partial(kernel, n, ni), out_shape=jax.ShapeDtype...  74.9 us
    unnamed x1, local copies, waits for them, and re-layouts  3.05 us

profile of v4, /device:TPU:19, one launch (start us, length us, event | category | flops | bytes accessed | tf_op | source)
XLA Modules:
  0.0 78.6 jit_solution(2297870290019632570)
XLA Ops:
  0.7 74.9 %shard_map.55 = f32[8,256,256]{2,1,0:T(8,128)} custom-call(bf16[16,1,80,1280]{3,2,1,0:T(8,128)(2,1)} %blocks.1, bf16[1280,1024]{1,0:T(8,128)(2,1)} %coef.1, s32[1280]{0:T(1024)} %batch.1, s32[1,1]{1,0:T(1,128)S(6)} %copy.7.sym, s32[8]{0:T(128)} %counts.1), custom_call_target="tpu_custom_call" | custom-call | tf_op jit(solution)/shard_map/pallas_call | solution.py:363
  75.5 3.0 %copy.8 = f32[1,1,8,256,256]{4,3,2,1,0:T(8,128)} copy(f32[1,1,8,256,256]{4,3,2,1,0:T(8,128)} %bitcast.1) | data formatting | bytes 4194304

commit v5 on v4

--- a/solution.py
+++ b/solution.py
@@ -212,11 +212,11 @@
                 make_rows_t(prev_slab)
             if relay and t == early:
                 pl.when(is_mid)(relay_early)
-    if relay:
-
-        @pl.when(is_end)
-        def _():
-            start(near_copies)
+            if relay and t == max(early - 1, 0):
+
+                @pl.when(is_end)
+                def _():
+                    start(near_copies)
 
     last, last_slab, _ = f_copies[-1]
     last.wait_recv()

time: 78.8 us -> 78.8 us (level)
  no operation moved by 1% of the time
where the time goes in v5:
time: 78.8 us; the launch traced here: 78.6 us
  Pallas kernels  74.9 us (95%)
  local copies, waits for them, and re-layouts  3.05 us (4%)
    pallas_call x1, Pallas kernels, body(): pl.pallas_call(functools.partial(kernel, n, ni), out_shape=jax.ShapeDtype...  74.9 us
    unnamed x1, local copies, waits for them, and re-layouts  3.05 us

profile of v5, /device:TPU:19, one launch (start us, length us, event | category | flops | bytes accessed | tf_op | source)
XLA Modules:
  0.0 78.6 jit_solution(6197670805637047855)
XLA Ops:
  0.7 74.9 %shard_map.55 = f32[8,256,256]{2,1,0:T(8,128)} custom-call(bf16[16,1,80,1280]{3,2,1,0:T(8,128)(2,1)} %blocks.1, bf16[1280,1024]{1,0:T(8,128)(2,1)} %coef.1, s32[1280]{0:T(1024)} %batch.1, s32[1,1]{1,0:T(1,128)S(6)} %copy.7.sym, s32[8]{0:T(128)} %counts.1), custom_call_target="tpu_custom_call" | custom-call | tf_op jit(solution)/shard_map/pallas_call | solution.py:363
  75.5 3.0 %copy.8 = f32[1,1,8,256,256]{4,3,2,1,0:T(8,128)} copy(f32[1,1,8,256,256]{4,3,2,1,0:T(8,128)} %bitcast.1) | data formatting | bytes 4194304
